TPU v7x, 256 devices: a whole 4x4x8 slice. The times are simulated.
256 devices in a mesh: ctx: 8 (over x, core), exp: 32 (over y, z).
Axes of the slice: x: 4, y: 4, z: 8, core: 2. Of those that a mesh axis runs over, the one named last changes fastest.
Arguments:
- tokens_in: bfloat16 [1024, 6144], P('ctx'), may hold values from -6 to 6
- queries: bfloat16 [1024, 8192], P('ctx', 'exp'), may hold values from -6 to 6
- keys: bfloat16 [1024, 8192], P('ctx', 'exp'), may hold values from -6 to 6
- values: bfloat16 [1024, 8192], P('ctx', 'exp'), may hold values from -6 to 6
- log_decay: float32 [64, 1024], P('exp', 'ctx'), may hold values from -1.3 to 0
- incoming_state: float32 [64, 128, 128], P('exp'), may hold values from -12 to 12
- attn_gain: float32 [8192], P('exp'), may hold values from 0.1 to 1.9
- w_out: bfloat16 [8192, 6144], P('exp'), may hold values from -0.0625 to 0.0625
- ffn_gain: float32 [6144], replicated, may hold values from 0.1 to 1.9
- router: bfloat16 [6144, 4], replicated, may hold values from -0.078125 to 0.078125
- expert_ids: int32 [1024, 2], P('ctx'), may hold values from 0 to 3, all different within a row; in each aligned block of 128 rows (0 to 127, 128 to 255, ...) at most 80 rows name the same one
- w_in: bfloat16 [2, 36864, 6144], P(None, ('exp', 'ctx')), may hold values from -0.078125 to 0.078125
- w_down: bfloat16 [36864, 6144], P(('exp', 'ctx')), may hold values from -0.0625 to 0.0625
Outputs:
- mixed: bfloat16 [1024, 6144], P('ctx', 'exp')
Inputs may be any that keep to these rules, and one draw needn't show every extreme that they name: `expert_ids`: A token's two experts differ. Among the 128 tokens of one index of ctx no expert is named by more than 80 tokens, a bound that some block reaches of them.
All inputs are finite; a program needn't handle non-finite values.
Results may differ from a plain program's by a relative error of at most 0.027.
Values may be sent and summed in bfloat16 or wider, within the bound.
A program may use at most 128 MiB of HBM per device.

v0:
```python
import jax
import jax.numpy as jnp
from jax import lax
from jax.sharding import PartitionSpec as P

FF = 9216
CAP = 80


HIGHEST = lax.Precision.HIGHEST
epsilon = 1e-06


def shifted(value, axis, steps):
    count = lax.axis_size(axis)
    initial, last = (max(0, -steps), min(count, count - steps))
    return lax.ppermute(value, axis, [(source, source + steps) for source in range(initial, last)])


def rms_scale(values_f32, gain):
    mean_square = jnp.mean(values_f32 * values_f32, axis=-1, keepdims=True)
    return values_f32 * lax.rsqrt(mean_square + epsilon) * gain


def local(
    tokens_in,
    queries,
    keys,
    values,
    log_decay,
    incoming_state,
    attn_gain,
    w_out,
    ffn_gain,
    router,
    expert_ids,
    w_in,
    w_down,
):
    row_count = queries.shape[0]
    head_count = incoming_state.shape[0]
    head_size = incoming_state.shape[1]
    scale = head_size ** (-0.5)
    q_heads = queries.reshape(row_count, head_count, head_size)
    k_heads = keys.reshape(row_count, head_count, head_size)
    v_float = values.reshape(row_count, head_count, head_size).astype(jnp.float32)
    cumulative = jnp.cumsum(log_decay, axis=1)
    decay_total = jnp.exp(cumulative[:, -1])
    tail = jnp.exp(cumulative[:, -1:] - cumulative)
    key_scaled = k_heads.astype(jnp.float32) * tail.T[:, :, None]
    local_state = jnp.einsum("thd,the->hde", key_scaled, v_float, precision=HIGHEST)
    leading = lax.axis_index("ctx") == 0
    state_in = jnp.where(leading, incoming_state, jnp.zeros_like(incoming_state))
    for hop_index in range(lax.axis_size("ctx") - 1):
        outgoing = decay_total[:, None, None] * state_in + local_state
        arrived = shifted(outgoing.astype(jnp.bfloat16), "ctx", 1).astype(outgoing.dtype)
        state_in = jnp.where(leading, incoming_state, arrived)
    positions = lax.iota(jnp.int32, row_count)
    lower = (positions[:, None] >= positions[None, :])[None, :, :]
    gap = jnp.where(lower, cumulative[:, :, None] - cumulative[:, None, :], 0.0)
    weight = jnp.where(lower, jnp.exp(gap), 0.0)
    scores = (
        jnp.einsum("thd,shd->hts", q_heads, k_heads, preferred_element_type=jnp.float32)
        * scale
        * weight
    )
    query_scaled = q_heads.astype(jnp.float32) * (scale * jnp.exp(cumulative)).T[:, :, None]
    attended = jnp.einsum("hts,she->the", scores, v_float, precision=HIGHEST) + jnp.einsum(
        "thd,hde->the", query_scaled, state_in, precision=HIGHEST
    )
    attn_heads = (
        rms_scale(attended, attn_gain.reshape(head_count, head_size))
        .astype(jnp.bfloat16)
        .reshape(row_count, head_count * head_size)
    )
    width = tokens_in.shape[1]
    exp_count = lax.axis_size("exp")
    attn_full = lax.psum(
        jnp.dot(attn_heads, w_out, preferred_element_type=jnp.float32).astype(jnp.bfloat16), "exp"
    ).astype(jnp.float32)
    mid_full = tokens_in.astype(jnp.float32) + attn_full
    normed = rms_scale(mid_full, ffn_gain).astype(jnp.bfloat16)
    expert_count = router.shape[1]
    logits = jnp.dot(normed, router, preferred_element_type=jnp.float32)
    picked = expert_ids[:, :, None] == lax.iota(jnp.int32, expert_count)[None, None, :]
    chosen = jnp.sum(jnp.where(picked, logits[:, None, :], 0.0), axis=2)
    sigmoid_gate = jax.nn.sigmoid(chosen)
    gates = sigmoid_gate / jnp.sum(sigmoid_gate, axis=1, keepdims=True)
    slice_units = w_in.shape[1]
    block_index = lax.axis_index("exp") * lax.axis_size("ctx") + lax.axis_index("ctx")
    owned = block_index * slice_units // FF
    paired = w_in.reshape(2 * slice_units, width)
    flat_routes = expert_ids.reshape(row_count * 2)
    one_hot = (flat_routes[:, None] == lax.iota(jnp.int32, expert_count)[None, :]).astype(jnp.int32)
    earlier_count = jnp.cumsum(one_hot, axis=0) - one_hot
    slot_of = jnp.sum(earlier_count * one_hot, axis=1).reshape(row_count, 2)
    capacity = CAP
    in_slot = (expert_ids == owned)[:, :, None] & (
        slot_of[:, :, None] == lax.iota(jnp.int32, capacity)[None, None, :]
    )
    placement = jnp.any(in_slot, axis=1).T.astype(jnp.bfloat16)
    slot_buffer = jnp.dot(placement, normed, preferred_element_type=jnp.float32).astype(
        jnp.bfloat16
    )
    combine = jnp.sum(jnp.where(in_slot, gates[:, :, None], 0.0), axis=1)
    projected = lax.dot_general(
        lax.all_gather(slot_buffer, "ctx", axis=0, tiled=True),
        paired,
        (((1,), (1,)), ((), ())),
        preferred_element_type=jnp.float32,
    )
    hidden = (jax.nn.silu(projected[:, :slice_units]) * projected[:, slice_units:]).astype(
        jnp.bfloat16
    )
    partials = jnp.dot(hidden, w_down, preferred_element_type=jnp.float32).astype(jnp.bfloat16)
    summed = lax.psum_scatter(
        partials.astype(jnp.float32).astype(jnp.bfloat16), "ctx", scatter_dimension=0, tiled=True
    ).astype(jnp.float32)
    contrib = jnp.dot(combine, summed, precision=HIGHEST)
    column_count = width // exp_count
    column_start = lax.axis_index("exp") * column_count
    residual = lax.dynamic_slice_in_dim(mid_full, column_start, column_count, 1)
    total = lax.psum_scatter(
        contrib.astype(jnp.bfloat16), "exp", scatter_dimension=1, tiled=True
    ).astype(jnp.float32)
    return (total + residual).astype(jnp.bfloat16)


def solution(mesh):
    return jax.shard_map(
        local,
        mesh=mesh,
        in_specs=(
            P("ctx", None),
            P("ctx", "exp"),
            P("ctx", "exp"),
            P("ctx", "exp"),
            P("exp", "ctx"),
            P("exp", None, None),
            P("exp"),
            P("exp", None),
            P(),
            P(),
            P("ctx", None),
            P(None, ("exp", "ctx"), None),
            P(("exp", "ctx"), None),
        ),
        out_specs=P("ctx", "exp"),
        check_vma=False,
    )
```

profile of v0, /device:TPU:1, one launch (start us, length us, event | category | flops | bytes accessed | tf_op | source)
XLA Modules:
  0.0 551.2 jit_solution(10375486550913919019)
XLA Ops:
  6.5 1.1 reduce_window_sum.28
  7.7 0.2 slice_reduce_fusion
  7.9 0.1 multiply_bitcast_fusion
  7.9 1.6 copy.73
  9.5 1.2 add_convert_fusion.7
  10.8 4.5 collective-permute-start
  15.3 1.3 collective-permute-done
  16.6 0.1 add_convert_fusion.6
  16.7 4.3 collective-permute-start.1
  21.0 1.3 collective-permute-done.1
  22.3 0.1 add_convert_fusion.5
  22.4 4.3 collective-permute-start.2
  26.6 1.3 collective-permute-done.2
  27.9 0.1 add_convert_fusion.4
  28.0 4.3 collective-permute-start.3
  32.3 1.3 collective-permute-done.3
  33.6 0.1 add_convert_fusion.3
  33.7 4.3 collective-permute-start.4
  38.0 1.3 collective-permute-done.4
  39.3 0.1 add_convert_fusion.2
  39.4 4.3 collective-permute-start.5
  43.7 1.0 fusion.1
  44.7 0.3 collective-permute-done.5
  45.0 0.1 add_convert_fusion.1
  45.1 4.3 collective-permute-start.6
  49.3 1.1 convolution_bitcast_fusion.1
  50.5 0.2 collective-permute-done.6
  50.7 0.5 multiply_reduce_fusion.1
  51.1 0.1 multiply_convert_fusion.1
  51.3 1.8 convolution_convert_fusion.2
  53.0 0.0 all-reduce.2.cloned.1.call-update
  53.0 0.0 all-gather.2.cloned.1.call-start
  53.1 0.7 copy.56
  53.9 1.0 eq.68
  54.8 1.0 eq.64
  55.8 1.2 reduce-window.6
  57.1 0.1 slice.21
  57.1 0.7 copy.58
  57.8 0.7 reduce-window.9
  58.5 0.6 slice.17
  59.1 0.8 copy.59
  59.8 0.1 add_bitcast_fusion
  59.9 0.8 eq.72
  60.7 0.9 copy.60
  61.6 0.5 copy-done.10
  62.1 142.1 %all-reduce.2.cloned.1.call-done = bf16[128,6144]{1,0:T(8,128)(2,1)} async-done(((bf16[128,6144]{1,0:T(8,128)(2,1)}), bf16[128,6144]{1,0:T(8,128)(2,1)}) %all-reduce.2.cloned.1.call-update) | async-done | bytes 1572880 | tf_op jit(solution)/shard_map/psum | solution.py:78
  204.2 4.3 multiply_reduce_fusion
  208.5 0.5 copy-done.13
  209.0 1.9 convolution_convert_fusion.3
  210.9 0.0 reduce-scatter.5.cloned.1.call-start
  211.0 51.8 %all-gather.2.cloned.1.call-done = bf16[640,6144]{1,0:T(8,128)(2,1)} async-done(((bf16[80,6144]{1,0:T(8,128)(2,1)}), bf16[640,6144]{1,0:T(8,128)(2,1)}) %all-gather.2.cloned.1.call-update) | async-done | bytes 7864336 | tf_op jit(solution)/shard_map/all_gather | solution.py:107
  262.8 5.4 fusion.31
  268.2 5.4 convolution_convert_fusion
  273.6 0.0 reduce-scatter.5.cloned.1.call-update
  273.6 0.0 reduce-scatter.7.cloned.1.call-start
  273.6 2.6 fusion.30
  276.3 0.6 select_reduce_fusion
  277.0 48.4 %reduce-scatter.5.cloned.1.call-done = bf16[80,6144]{1,0:T(8,128)(2,1)} async-done(((bf16[640,6144]{1,0:T(8,128)(2,1)}), bf16[80,6144]{1,0:T(8,128)(2,1)}) %reduce-scatter.5.cloned.1.call-update) | async-done | bytes 983056 | tf_op jit(solution)/shard_map/reduce_scatter | solution.py:116
  325.4 4.1 fusion
  329.6 0.0 reduce-scatter.7.cloned.1.call-update
  329.6 210.3 %reduce-scatter.7.cloned.1.call-done = bf16[192,128]{1,0:T(8,128)(2,1)} async-done(((bf16[6144,128]{1,0:T(8,128)(2,1)}), bf16[192,128]{1,0:T(8,128)(2,1)}) %reduce-scatter.7.cloned.1.call-update) | async-done | bytes 49168
  539.9 1.5 copy.72
  541.4 1.7 add_convert_fusion
  543.1 1.6 copy.69
  (39 shorter events, 0.2 us)
Async XLA Ops:
  6.5 256.2 %copy-start = (bf16[2,144,6144]{2,1,0:T(8,128)(2,1)S(1)}, bf16[2,144,6144]{2,1,0:T(8,128)(2,1)}, u32[]{:S(2)}) copy-start(bf16[2,144,6144]{2,1,0:T(8,128)(2,1)} %param.24) | copy-start | bytes 10616836
  6.5 197.6 %all-reduce.2.cloned.1.call-start = ((), (), s32[]{:S(2)}) async-start(), calls=%async_computation.2 | async-start | bytes 3145728 | tf_op jit(solution)/shard_map/psum | solution.py:78
  9.5 41.1 %copy-start.1 = (f32[2,128,128]{2,1,0:T(8,128)S(1)}, f32[2,128,128]{2,1,0:T(8,128)}, u32[]{:S(2)}) copy-start(f32[2,128,128]{2,1,0:T(8,128)} %param.18) | copy-start | bytes 393220
  9.5 41.1 %copy-start.6 = (bf16[128,256]{1,0:T(8,128)(2,1)S(1)}, bf16[128,256]{1,0:T(8,128)(2,1)}, u32[]{:S(2)}) copy-start(bf16[128,256]{1,0:T(8,128)(2,1)} %param.14) | copy-start | bytes 196612
  9.5 41.6 %copy-start.12 = (f32[256]{0:T(256)S(1)}, f32[256]{0:T(256)}, u32[]{:S(2)}) copy-start(f32[256]{0:T(256)} %param.19) | copy-start | bytes 3076
  9.5 41.7 %copy-start.4 = (bf16[256,6144]{1,0:T(8,128)(2,1)S(1)}, bf16[256,6144]{1,0:T(8,128)(2,1)}, u32[]{:S(2)}) copy-start(bf16[256,6144]{1,0:T(8,128)(2,1)} %param.20) | copy-start | bytes 9437188
  10.8 5.8 %collective-permute-start = (bf16[2,128,128]{2,1,0:T(8,128)(2,1)S(1)}, bf16[2,128,128]{2,1,0:T(8,128)(2,1)S(1)}, u32[]{:S(2)}, u32[]{:S(2)}) collective-permute-start(bf16[2,128,128]{2,1,0:T(8,128)(2,1)S(1)} %get-tuple-element.9), channel_id=1, source_target_pairs={{0,32},{32,64},{64,96},{96,128},{128,160},{160,192},{192,224},{1,3... | collective-permute-start | bytes 196616 | tf_op jit(solution)/shard_map/ppermute | solution.py:17
  16.7 5.6 %collective-permute-start.1 = (bf16[2,128,128]{2,1,0:T(8,128)(2,1)S(1)}, bf16[2,128,128]{2,1,0:T(8,128)(2,1)S(1)}, u32[]{:S(2)}, u32[]{:S(2)}) collective-permute-start(bf16[2,128,128]{2,1,0:T(8,128)(2,1)S(1)} %add_convert_fusion.6), channel_id=1, source_target_pairs={{0,32},{32,64},{64,96},{96,128},{128,160},{160,192},{192,224},{1,3... | collective-permute-start | bytes 196616 | tf_op jit(solution)/shard_map/ppermute | solution.py:17
  22.4 5.6 %collective-permute-start.2 = (bf16[2,128,128]{2,1,0:T(8,128)(2,1)S(1)}, bf16[2,128,128]{2,1,0:T(8,128)(2,1)S(1)}, u32[]{:S(2)}, u32[]{:S(2)}) collective-permute-start(bf16[2,128,128]{2,1,0:T(8,128)(2,1)S(1)} %add_convert_fusion.5), channel_id=1, source_target_pairs={{0,32},{32,64},{64,96},{96,128},{128,160},{160,192},{192,224},{1,3... | collective-permute-start | bytes 196616 | tf_op jit(solution)/shard_map/ppermute | solution.py:17
  28.0 5.6 %collective-permute-start.3 = (bf16[2,128,128]{2,1,0:T(8,128)(2,1)S(1)}, bf16[2,128,128]{2,1,0:T(8,128)(2,1)S(1)}, u32[]{:S(2)}, u32[]{:S(2)}) collective-permute-start(bf16[2,128,128]{2,1,0:T(8,128)(2,1)S(1)} %add_convert_fusion.4), channel_id=1, source_target_pairs={{0,32},{32,64},{64,96},{96,128},{128,160},{160,192},{192,224},{1,3... | collective-permute-start | bytes 196616 | tf_op jit(solution)/shard_map/ppermute | solution.py:17
  33.7 5.6 %collective-permute-start.4 = (bf16[2,128,128]{2,1,0:T(8,128)(2,1)S(1)}, bf16[2,128,128]{2,1,0:T(8,128)(2,1)S(1)}, u32[]{:S(2)}, u32[]{:S(2)}) collective-permute-start(bf16[2,128,128]{2,1,0:T(8,128)(2,1)S(1)} %add_convert_fusion.3), channel_id=1, source_target_pairs={{0,32},{32,64},{64,96},{96,128},{128,160},{160,192},{192,224},{1,3... | collective-permute-start | bytes 196616 | tf_op jit(solution)/shard_map/ppermute | solution.py:17
  39.4 5.6 %collective-permute-start.5 = (bf16[2,128,128]{2,1,0:T(8,128)(2,1)S(1)}, bf16[2,128,128]{2,1,0:T(8,128)(2,1)S(1)}, u32[]{:S(2)}, u32[]{:S(2)}) collective-permute-start(bf16[2,128,128]{2,1,0:T(8,128)(2,1)S(1)} %add_convert_fusion.2), channel_id=1, source_target_pairs={{0,32},{32,64},{64,96},{96,128},{128,160},{160,192},{192,224},{1,3... | collective-permute-start | bytes 196616 | tf_op jit(solution)/shard_map/ppermute | solution.py:17
  45.1 5.6 %collective-permute-start.6 = (bf16[2,128,128]{2,1,0:T(8,128)(2,1)S(1)}, bf16[2,128,128]{2,1,0:T(8,128)(2,1)S(1)}, u32[]{:S(2)}, u32[]{:S(2)}) collective-permute-start(bf16[2,128,128]{2,1,0:T(8,128)(2,1)S(1)} %add_convert_fusion.1), channel_id=1, source_target_pairs={{0,32},{32,64},{64,96},{96,128},{128,160},{160,192},{192,224},{1,3... | collective-permute-start | bytes 196616 | tf_op jit(solution)/shard_map/ppermute | solution.py:17
  51.2 1.9 copy-start.8
  53.0 209.7 %all-gather.2.cloned.1.call-start = ((), (), s32[]{:S(2)}) async-start(), calls=%async_computation.3 | async-start | bytes 8847360 | tf_op jit(solution)/shard_map/all_gather | solution.py:107
  61.6 0.5 copy-start.10
  204.2 4.8 copy-start.2
  204.2 4.8 copy-start.3
  204.2 4.8 copy-start.7
  208.5 0.5 copy-start.13
  210.9 114.5 %reduce-scatter.5.cloned.1.call-start = ((), (), s32[]{:S(2)}) async-start(), calls=%async_computation.4 | async-start | bytes 8847360 | tf_op jit(solution)/shard_map/reduce_scatter | solution.py:116
  262.8 5.4 copy-start.5
  273.6 2.7 copy-start.9
  273.6 2.7 copy-start.11
  273.6 266.3 %reduce-scatter.7.cloned.1.call-start = ((), (), s32[]{:S(2)}) async-start(), calls=%async_computation.5 | async-start | bytes 1622016
Sparse Core Ops, SparseCore 0:
  53.2 150.9 all-reduce.1
  211.0 51.6 all-gather.1
  273.7 51.6 reduce-scatter.4
  329.7 210.1 reduce-scatter.6
where the time goes:
time: 556 us; the launch traced here: 551 us
  waiting for transfers between devices  460 us (83%)
  starting transfers between devices  30.2 us (5%)
  matrix products  25 us (4%)
  between operations  13.4 us (2%)
  local copies, waits for them, and re-layouts  12.3 us (2%)
  other arithmetic  10.6 us (2%)
    unnamed x5, waiting for transfers between devices  210 us
    psum x1, waiting for transfers between devices, local(): lax.psum(jnp.dot(attn_heads, w_out, preferred_element_type=jnp.float32).a...  142 us
    all_gather x1, waiting for transfers between devices, local(): lax.all_gather(slot_buffer, 'ctx', axis=0, tiled=True)  51.8 us
    reduce_scatter x1, waiting for transfers between devices, local(): lax.psum_scatter(partials.astype(jnp.float32).astype(jnp.bfloat16), 'ctx'...  48.4 us
    ppermute x7, starting transfers between devices, shifted(): lax.ppermute(value, axis, [(source, source + steps) for source in range(i...  30.1 us
  transfers between devices with their start and end apart: 11, of which 11 were waited for; matrix products, arithmetic and copies ran while one was open for 3% of the time, Pallas kernels for 0%

commit v1 on v0

v1 whole, which is shorter than its diff:
```python
import functools

import jax
import jax.numpy as jnp
from jax import lax
from jax.experimental import pallas as pl
from jax.experimental.pallas import tpu as pltpu
from jax.sharding import PartitionSpec as P

MESH = pl.DeviceIdType.MESH
HI = lax.Precision.HIGHEST
F32 = jnp.float32
BF = jnp.bfloat16
EPS = 1e-06

D = 6144
T = 128
HD = 128
CAP = 80
SL = 144
HALF = D // 2
FB = HALF // 8
OUT = D // 32

HOPS = ((4, 4, 3, 3), (3, 3, 4, 4))
HOPB = (4, 3)


def nt(a, b, precision=None):
    return lax.dot_general(
        a, b, (((1,), (1,)), ((), ())), preferred_element_type=F32, precision=precision
    )


def nn(a, b, precision=None):
    return jnp.dot(a, b, preferred_element_type=F32, precision=precision)


def iota2(shape, dim):
    return lax.broadcasted_iota(jnp.int32, shape, dim)


def kernel(
    tok_ref,
    q_ref,
    k_ref,
    v_ref,
    ld_ref,
    inc_ref,
    ag_ref,
    wo_ref,
    fg_ref,
    ro_ref,
    ids_ref,
    wi_ref,
    wd_ref,
    out_ref,
    WO, WI, WD, RO, TK, IDS,
    LS, TS, LB, TB, ST, WR,
    AH, PP, A1R, QQ, A2R, A3R, MID,
    PL, SR, LG, RX, XG, ACC, PS, PR, HID,
    YY, RBA, RBB, XRA, XRB, YS, FS, FR,
    loc, sib_s, sib_r, st_s, st_r, tt_s, tt_r,
    a1_s, a1_r, a2_s, a2_r, a3_s, a3_r, sx_s, sx_r, rx_s, rx_r,
    pr_s, pr_r, ax_s, ax_r, ar_s, ar_r, br_s, br_r, bx_s, bx_r,
    ra_s, ra_r, rr_s, rr_r, rb_s, rb_r, rx2_s, rx2_r, fn_s, fn_r,
):
    c = lax.axis_index("ctx")
    e = lax.axis_index("exp")
    x, k = c // 2, lax.rem(c, 2)
    y, z = e // 8, lax.rem(e, 8)
    b = k * 8 + z
    pend = []

    def xx(d):
        return lax.rem(x + (d + 8), 4)

    def yv(d):
        return lax.rem(y + (d + 8), 4)

    def zz(o):
        return lax.rem(z + (o + 16), 8)

    def send(src, dst, ss, rs, dc, de, keep=True):
        cp = pltpu.make_async_remote_copy(
            src_ref=src, dst_ref=dst, send_sem=ss, recv_sem=rs,
            device_id=(dc, de), device_id_type=MESH,
        )
        cp.start()
        if keep:
            pend.append(cp)
        return cp

    def arrive(dst, ss, rs):
        pltpu.make_async_remote_copy(
            src_ref=dst, dst_ref=dst, send_sem=ss, recv_sem=rs,
            device_id=(c, e), device_id_type=MESH,
        ).wait_recv()

    def cols(i, n):
        return pl.ds(pl.multiple_of(i * n, 128), n)

    bar = pltpu.get_barrier_semaphore()

    def hello(dc, de):
        pl.semaphore_signal(bar, inc=1, device_id=(dc, de), device_id_type=MESH)

    sibling = 2 * x + (1 - k)
    for d in range(1, 8):
        hello(lax.rem(c + d, 8), e)
    for d in range(1, 4):
        hello(c, yv(d) * 8 + z)
    for o in range(1, 8):
        hello(c, y * 8 + zz(o))
        hello(sibling, y * 8 + zz(o))
    src_b = e // 2
    src_k, src_z = src_b // 8, lax.rem(src_b, 8)
    src_mine = (src_k == k) & (src_z == z)
    for yy in range(4):
        @pl.when(jnp.logical_not(src_mine & (y == yy)))
        def _(yy=yy):
            hello(2 * x + src_k, yy * 8 + src_z)
    lc_wo = pltpu.make_async_copy(wo_ref, WO, loc.at[0])
    lc_wo.start()
    lc_tk = pltpu.make_async_copy(tok_ref.at[:, cols(b, FB)], TK.at[k], loc.at[1])
    lc_tk.start()
    lc_ro = pltpu.make_async_copy(
        ro_ref.at[pl.ds(pl.multiple_of(b * FB, 16), FB)], RO, loc.at[2]
    )
    lc_ro.start()

    row_i = iota2((T, T), 0)
    col_i = iota2((T, T), 1)
    lower = row_i >= col_i
    scale = HD ** (-0.5)
    cums = []
    for h in range(2):
        hs = slice(h * HD, (h + 1) * HD)
        ld = ld_ref[h:h + 1, :]
        cum = jnp.sum(jnp.where(lower, ld, 0.0), axis=1, keepdims=True)
        tot = jnp.sum(ld, axis=1, keepdims=True)
        cums.append(cum)
        ks = k_ref[:, hs].astype(F32) * jnp.exp(tot - cum)
        LS[h] = nn(ks.T, v_ref[:, hs].astype(F32), HI).astype(BF)
        TS[h:h + 1, :] = jnp.broadcast_to(tot, (1, T))
    TS[2:, :] = jnp.zeros((6, T), F32)
    idc = ids_ref[...].astype(F32)
    ident = row_i == col_i
    r0 = jnp.sum(jnp.where(ident, idc[:, 0:1], 0.0), axis=0, keepdims=True)
    r1 = jnp.sum(jnp.where(ident, idc[:, 1:2], 0.0), axis=0, keepdims=True)
    sub8 = iota2((8, T), 0)
    IDS[k] = jnp.where(sub8 == 0, r0, jnp.where(sub8 == 1, r1, 0.0))

    pl.semaphore_wait(bar, 28 - (src_mine).astype(jnp.int32))

    for d in range(1, 8):
        @pl.when(c + d < 8)
        def _(d=d):
            send(TS, TB.at[d - 1], tt_s.at[d - 1], tt_r.at[d - 1], c + d, e, False)
            send(LS, LB.at[d - 1], st_s.at[d - 1], st_r.at[d - 1], c + d, e, False)

    ob = (1 - k) * 8 + z
    send(tok_ref.at[:, cols(ob, FB)], TK.at[k], sib_s.at[0], sib_r.at[0], sibling, e)
    send(IDS.at[k], IDS.at[k], sib_s.at[1], sib_r.at[1], sibling, e)
    mine, other = cols(k, HALF), cols(1 - k, HALF)
    lc_wi = pltpu.make_async_copy(wi_ref.at[:, :, mine], WI.at[k], loc.at[3])
    lc_wi.start()
    lc_wd = pltpu.make_async_copy(wd_ref.at[:, mine], WD.at[k], loc.at[4])
    lc_wd.start()
    send(wi_ref.at[:, :, other], WI.at[k], sib_s.at[2], sib_r.at[2], sibling, e)
    send(wd_ref.at[:, other], WD.at[k], sib_s.at[3], sib_r.at[3], sibling, e)

    intra, qsc = [], []
    for h in range(2):
        hs = slice(h * HD, (h + 1) * HD)
        cum = cums[h]
        cb = jnp.broadcast_to(cum, (T, T))
        gap = jnp.where(lower, cb - cb.T, 0.0)
        weight = jnp.where(lower, jnp.exp(gap), 0.0)
        sc = nt(q_ref[:, hs], k_ref[:, hs]) * scale * weight
        intra.append(nn(sc, v_ref[:, hs].astype(F32), HI))
        qsc.append(q_ref[:, hs].astype(F32) * (scale * jnp.exp(cum)))

    ST[...] = jnp.zeros_like(ST)
    WR[...] = jnp.zeros_like(WR)
    for d in range(1, 8):
        @pl.when(c >= d)
        def _(d=d):
            arrive(TB.at[d - 1], tt_s.at[d - 1], tt_r.at[d - 1])
            arrive(LB.at[d - 1], st_s.at[d - 1], st_r.at[d - 1])
            for h in range(2):
                ST[h] = ST[h] + jnp.exp(WR[h:h + 1, :]) * LB[d - 1, h].astype(F32)
            WR[...] = WR[...] + TB[d - 1]
    for h in range(2):
        hs = slice(h * HD, (h + 1) * HD)
        state = ST[h] + jnp.exp(WR[h:h + 1, :]) * inc_ref[h]
        att = intra[h] + nn(qsc[h], state, HI)
        ms = jnp.mean(att * att, axis=1, keepdims=True)
        AH[:, hs] = (att * lax.rsqrt(ms + EPS) * ag_ref[h:h + 1, :]).astype(BF)

    lc_wo.wait()
    for kc in range(2):
        def project(i, carry, kc=kc):
            cs = pl.ds(pl.multiple_of(kc * HALF + i * 512, 128), 512)
            PP[:, cs] = nn(AH[...], WO[:, cs]).astype(BF)
            return carry
        lax.fori_loop(0, HALF // 512, project, 0)
        for d in (2, 1, 3):
            i = kc * 3 + d - 1
            cs = slice(kc * HALF, (kc + 1) * HALF)
            send(
                PP.at[pl.ds(pl.multiple_of(yv(d) * 32, 32), 32), cs],
                A1R.at[d - 1, :, cs],
                a1_s.at[i], a1_r.at[i], c, yv(d) * 8 + z,
            )
    for kc in range(2):
        cs = slice(kc * HALF, (kc + 1) * HALF)
        for d in range(1, 4):
            i = kc * 3 + d - 1
            arrive(A1R.at[d - 1, :, cs], a1_s.at[i], a1_r.at[i])

        def add_y(i, carry, kc=kc):
            s = pl.ds(pl.multiple_of(kc * HALF + i * 512, 128), 512)
            acc = PP[pl.ds(pl.multiple_of(y * 32, 32), 32), s].astype(F32)
            for d in range(3):
                acc = acc + A1R[d, :, s].astype(F32)
            QQ[:, s] = acc.astype(BF)
            return carry
        lax.fori_loop(0, HALF // 512, add_y, 0)
        dest = 2 * x + kc
        for o in (4, 3, 5, 2, 6, 1, 7):
            send(
                QQ.at[:, cols(kc * 8 + zz(o), FB)],
                A2R.at[k, o], a2_s.at[kc, o], a2_r.at[k, o], dest, y * 8 + zz(o),
            )
        own = cols(kc * 8 + z, FB)

        @pl.when(k == kc)
        def _(own=own):
            A2R[k, 0] = QQ[:, own]

        @pl.when(k != kc)
        def _(own=own, kc=kc, dest=dest):
            send(QQ.at[:, own], A2R.at[k, 0], a2_s.at[kc, 0], a2_r.at[k, 0], dest, e, False)

    for kc in range(2):
        @pl.when(k != kc)
        def _(kc=kc):
            arrive(A2R.at[kc, 0], a2_s.at[kc, 0], a2_r.at[kc, 0])
        acc = A2R[kc, 0].astype(F32)
        for o in range(1, 8):
            arrive(A2R.at[kc, o], a2_s.at[kc, o], a2_r.at[kc, o])
            acc = acc + A2R[kc, o].astype(F32)
        A3R[0, kc] = acc.astype(BF)
    for d in range(1, 4):
        send(A3R.at[0], A3R.at[d], a3_s.at[d - 1], a3_r.at[d - 1], c, yv(d) * 8 + z)

    arrive(IDS.at[1 - k], sib_s.at[1], sib_r.at[1])
    strict = (row_i < col_i).astype(BF)
    yf = y.astype(F32)
    for kc in range(2):
        mask = ((IDS[kc, 0:1, :] == yf) | (IDS[kc, 1:2, :] == yf)).astype(F32)
        before = nn(jnp.broadcast_to(mask, (8, T)).astype(BF), strict)[0:1, :]
        PL[kc] = jnp.where(
            (row_i.astype(F32) == before) & (row_i < CAP), mask, 0.0
        )

    lc_tk.wait()
    arrive(TK.at[1 - k], sib_s.at[0], sib_r.at[0])
    lc_ro.wait()
    gain = jnp.concatenate([fg_ref[pl.ds(b * 3 + i, 1), :] for i in range(3)], axis=1)
    for d in range(4):
        if d:
            arrive(A3R.at[d], a3_s.at[d - 1], a3_r.at[d - 1])
        rows = pl.ds(pl.multiple_of(yv(-d) * 32, 32), 32)
        for kc in range(2):
            MID[kc, rows, :] = TK[kc, rows, :].astype(F32) + A3R[d, kc].astype(F32)

    def rows_a(i):
        return pl.ds(pl.multiple_of(i * 160, 16), 80)

    def rows_b(i):
        return pl.ds(pl.multiple_of(i * 160 + 80, 16), 80)

    def piece_a(zs, d):
        return XG.at[zs, rows_a(xx(-d))]

    def piece_b(zs, d):
        return XG.at[zs, rows_b(xx(-d))]

    step_dir = (1, -1)

    def alpha_ring(r, d, h):
        p = piece_a(zz(-step_dir[r] * (h - 1)), d)
        send(p, p, ar_s.at[r, d, h - 1], ar_r.at[r, d, h - 1], c, y * 8 + zz(step_dir[r]))

    def beta_ring(r, h):
        p = piece_b(zz(-step_dir[r] * (h - 1)), 0)
        send(p, p, br_s.at[r, h - 1], br_r.at[r, h - 1], c, y * 8 + zz(step_dir[r]))

    def beta_x(o):
        p = piece_b(zz(o), 0)
        for d in range(1, 4):
            send(p, p, bx_s.at[o % 8, d - 1], bx_r.at[o % 8, d - 1], 2 * xx(d) + k, e)

    def beta_x_wait(o):
        for d in range(1, 4):
            arrive(piece_b(zz(o), d), bx_s.at[o % 8, d - 1], bx_r.at[o % 8, d - 1])

    for kc in (1, 0):
        xg = (MID[kc] * gain).astype(BF)
        slots = nn(PL[kc, :CAP, :].astype(BF), xg).astype(BF)
        if kc:
            XG[z, rows_b(x), :] = slots
            beta_ring(0, 1)
            beta_ring(1, 1)
        else:
            XG[z, rows_a(x), :] = slots
            pa = piece_a(z, 0)
            for d in range(1, 4):
                send(pa, pa, ax_s.at[d - 1], ax_r.at[d - 1], 2 * xx(d) + k, e)
            alpha_ring(0, 0, 1)
            alpha_ring(1, 0, 1)
            beta_x(0)
    lane = iota2((T, T), 1)
    for kc in range(2):
        m = MID[kc]
        lg = nn((m * gain).astype(BF), RO[...])
        st = jnp.where(lane == 4, jnp.sum(m * m, axis=1, keepdims=True), 0.0)
        for j in range(4):
            st = jnp.where(lane == j, lg[:, j:j + 1], st)
        SR[0, :, kc * T:(kc + 1) * T] = st.T[0:8, :]
    for o in range(16):
        if o:
            dk = o // 8
            send(
                SR.at[0], SR.at[o], sx_s.at[o], sx_r.at[o],
                sibling if dk else c, y * 8 + zz(o % 8),
            )

    lc_wi.wait()
    arrive(WI.at[1 - k], sib_s.at[2], sib_r.at[2])

    def ffn_in(o, first=False):
        zs = zz(o)
        ws = cols(zs, FB)

        def body(i, carry):
            rows = pl.ds(pl.multiple_of(i * 160, 16), 160)
            xb = XG[zs, rows, :]
            for q in range(4):
                r = nt(xb, WI[q // 2, q % 2, :, ws])
                if first:
                    ACC[q, rows, :] = r
                else:
                    ACC[q, rows, :] = ACC[q, rows, :] + r
            return carry
        lax.fori_loop(0, 4, body, 0)

    for h in range(1, 5):
        for r in range(2):
            if h <= HOPB[r]:
                arrive(piece_b(zz(-step_dir[r] * h), 0), br_s.at[r, h - 1], br_r.at[r, h - 1])
                if h < HOPB[r]:
                    beta_ring(r, h + 1)
                beta_x(-step_dir[r] * h)
        for d in range(4):
            if h == 1 and d:
                arrive(piece_a(z, d), ax_s.at[d - 1], ax_r.at[d - 1])
                alpha_ring(0, d, 1)
                alpha_ring(1, d, 1)
        for d in range(4):
            for r in range(2):
                if h <= HOPS[r][d]:
                    arrive(
                        piece_a(zz(-step_dir[r] * h), d),
                        ar_s.at[r, d, h - 1], ar_r.at[r, d, h - 1],
                    )
                    if h < HOPS[r][d]:
                        alpha_ring(r, d, h + 1)
        if h == 1:
            beta_x_wait(0)
            ffn_in(0, True)
            for o in range(1, 16):
                arrive(SR.at[o], sx_s.at[o], sx_r.at[o])
            tot = SR[0]
            for o in range(1, 16):
                tot = tot + SR[o]
            rstd = lax.rsqrt(tot[4:5, :] / D + EPS)
            LG[...] = tot * rstd
            rs = jnp.concatenate(
                [
                    nt(jnp.broadcast_to(rstd[:, kc * T:(kc + 1) * T], (8, T)), PL[kc], HI)
                    for kc in range(2)
                ],
                axis=1,
            )
            RX[0] = rs
            for d in range(1, 4):
                send(RX.at[0], RX.at[d], rx_s.at[d - 1], rx_r.at[d - 1], 2 * xx(d) + k, e)
        else:
            for o in (h - 1, 1 - h):
                beta_x_wait(o)
                ffn_in(o)
    beta_x_wait(-4)
    ffn_in(-4)

    for g in range(2):
        PS[g] = ACC[2 * (1 - k) + g].astype(BF)
    send(PS, PR, pr_s.at[0], pr_r.at[0], sibling, e)
    for d in range(1, 4):
        arrive(RX.at[d], rx_s.at[d - 1], rx_r.at[d - 1])
    lc_wd.wait()
    arrive(WD.at[1 - k], sib_s.at[3], sib_r.at[3])
    arrive(PR, pr_s.at[0], pr_r.at[0])
    for d in range(4):
        for kc in range(2):
            rs = RX[d, 0:1, kc * T:(kc + 1) * T]
            col = jnp.broadcast_to(rs, (T, T)).T[:CAP, 0:1]
            rows = (rows_b if kc else rows_a)(xx(-d))
            g = (ACC[2 * k, rows, :] + PR[0, rows, :].astype(F32)) * col
            u = (ACC[2 * k + 1, rows, :] + PR[1, rows, :].astype(F32)) * col
            HID[k, rows, :] = (g / (1.0 + jnp.exp(-g)) * u).astype(BF)
    send(HID.at[k], HID.at[k], pr_s.at[1], pr_r.at[1], sibling, e)
    arrive(HID.at[1 - k], pr_s.at[1], pr_r.at[1])

    def down(o):
        zs = zz(o)
        ws = cols(zs, FB)

        def body(i, carry):
            rows = pl.ds(pl.multiple_of(i * 160, 16), 160)
            r = nn(HID[0, rows, :], WD[0, :, ws]) + nn(HID[1, rows, :], WD[1, :, ws])
            YY[zs, rows, :] = r.astype(BF)
            return carry
        lax.fori_loop(0, 4, body, 0)

    def back_ring(r, d, s):
        hops = HOPS[r][d]
        zs = zz(step_dir[r] * (hops - s))
        p = YY.at[zs, rows_a(xx(d))]
        if s:
            arrive(RBA.at[r, d, s - 1], rr_s.at[r, d, s - 1], rr_r.at[r, d, s - 1])
            p[...] = (p[...].astype(F32) + RBA[r, d, s - 1].astype(F32)).astype(BF)
        send(p, RBA.at[r, d, s], rr_s.at[r, d, s], rr_r.at[r, d, s], c, y * 8 + zz(step_dir[r]))

    def back_x(o):
        for d in range(1, 4):
            send(
                YY.at[zz(o), rows_b(xx(d))], XRB.at[o % 8, d - 1],
                rx2_s.at[o % 8, d - 1], rx2_r.at[o % 8, d - 1], 2 * xx(d) + k, e,
            )

    def back_x_sum(o):
        acc = YY[zz(o), rows_b(x), :].astype(F32)
        for d in range(1, 4):
            arrive(XRB.at[o % 8, d - 1], rx2_s.at[o % 8, d - 1], rx2_r.at[o % 8, d - 1])
            acc = acc + XRB[o % 8, d - 1].astype(F32)
        return acc

    def back_ring_b(r, s):
        o = step_dir[r] * (HOPB[r] - s)
        acc = back_x_sum(o)
        if s:
            arrive(RBB.at[r, s - 1], rb_s.at[r, s - 1], rb_r.at[r, s - 1])
            acc = acc + RBB[r, s - 1].astype(F32)
        p = YY.at[zz(o), rows_b(x)]
        p[...] = acc.astype(BF)
        send(p, RBB.at[r, s], rb_s.at[r, s], rb_r.at[r, s], c, y * 8 + zz(step_dir[r]))

    for o in (4, 3, -3, -2, 2, -1, 1, 0):
        down(o)
        for r in range(2):
            for d in range(4):
                if (step_dir[r] * HOPS[r][d] - o) % 8 == 0:
                    back_ring(r, d, 0)
        back_x(o)
    for s in range(1, 5):
        for d in range(4):
            for r in range(2):
                if s < HOPS[r][d]:
                    back_ring(r, d, s)
        for r in range(2):
            if s - 1 < HOPB[r]:
                back_ring_b(r, s - 1)
    for d in (2, 1, 3, 0):
        acc = YY[z, rows_a(xx(d)), :].astype(F32)
        for r in range(2):
            s = HOPS[r][d] - 1
            arrive(RBA.at[r, d, s], rr_s.at[r, d, s], rr_r.at[r, d, s])
            acc = acc + RBA[r, d, s].astype(F32)
        if d:
            p = YY.at[z, rows_a(xx(d))]
            p[...] = acc.astype(BF)
            send(p, XRA.at[d - 1], ra_s.at[d - 1], ra_r.at[d - 1], 2 * xx(d) + k, e)
        else:
            YS[0, :CAP, :] = acc
    acc = back_x_sum(0)
    for r in range(2):
        s = HOPB[r] - 1
        arrive(RBB.at[r, s], rb_s.at[r, s], rb_r.at[r, s])
        acc = acc + RBB[r, s].astype(F32)
    YS[1, :CAP, :] = acc
    acc = YS[0, :CAP, :]
    for d in range(1, 4):
        arrive(XRA.at[d - 1], ra_s.at[d - 1], ra_r.at[d - 1])
        acc = acc + XRA[d - 1].astype(F32)
    YS[0, :CAP, :] = acc

    first = (y == 0).astype(F32)
    target = 2 * b
    to_me = (target == e) | (target + 1 == e)
    for kc in range(2):
        sg = 1.0 / (1.0 + jnp.exp(-LG[:, kc * T:(kc + 1) * T]))
        i0, i1 = IDS[kc, 0:1, :], IDS[kc, 1:2, :]
        den = jnp.zeros((1, T), F32)
        num = jnp.zeros((1, T), F32)
        for j in range(4):
            hit = ((i0 == j) | (i1 == j)).astype(F32) * sg[j:j + 1, :]
            den = den + hit
            num = num + jnp.where(y == j, hit, 0.0)
        gate = num / den
        got = nn((PL[kc] * gate).T[:, :CAP], YS[kc, :CAP, :], HI)
        got = got + first * MID[kc]
        for j in range(2):
            FS[kc * 2 + j] = got[:, j * OUT:(j + 1) * OUT].astype(BF)
            dc, de = 2 * x + kc, target + j
            is_me = (k == kc) & (de == e)

            @pl.when(is_me)
            def _(i=kc * 2 + j):
                FR[y] = FS[i]

            @pl.when(jnp.logical_not(is_me))
            def _(i=kc * 2 + j, dc=dc, de=de):
                send(FS.at[i], FR.at[y], fn_s.at[i], fn_r.at[y], dc, de, False)

    for yy in range(4):
        @pl.when(jnp.logical_not(src_mine & (y == yy)))
        def _(yy=yy):
            arrive(FR.at[yy], fn_s.at[yy], fn_r.at[yy])
    acc = FR[0].astype(F32)
    for yy in range(1, 4):
        acc = acc + FR[yy].astype(F32)
    out_ref[...] = acc.astype(BF)

    def left(src, ss):
        pltpu.make_async_remote_copy(
            src_ref=src, dst_ref=src, send_sem=ss, recv_sem=ss,
            device_id=(c, e), device_id_type=MESH,
        ).wait_send()

    for cp in pend:
        cp.wait_send()
    for d in range(1, 8):
        @pl.when(c + d < 8)
        def _(d=d):
            left(TS, tt_s.at[d - 1])
            left(LS, st_s.at[d - 1])
    for kc in range(2):
        @pl.when(k != kc)
        def _(kc=kc):
            left(QQ.at[:, cols(kc * 8 + z, FB)], a2_s.at[kc, 0])
        for j in range(2):
            @pl.when(jnp.logical_not((k == kc) & (target + j == e)))
            def _(i=kc * 2 + j):
                left(FS.at[i], fn_s.at[i])


def local(tok, q, kk, v, ld, inc, ag, wo, fg, ro, ids, wi, wd):
    vm = lambda *s, t=BF: pltpu.VMEM(s, t)
    dma = lambda *s: pltpu.SemaphoreType.DMA(s)
    inside = pl.BlockSpec(memory_space=pltpu.VMEM)
    outside = pl.BlockSpec(memory_space=pl.ANY)
    scratch = [
        vm(256, D), vm(2, 2, SL, HALF), vm(2, SL, HALF), vm(FB, 4), vm(2, T, FB), vm(2, 8, T, t=F32),
        vm(2, HD, HD), vm(8, T, t=F32), vm(7, 2, HD, HD), vm(7, 8, T, t=F32),
        vm(2, HD, HD, t=F32), vm(8, T, t=F32),
        vm(T, 2 * HD), vm(T, D), vm(3, 32, D), vm(32, D), vm(2, 8, 32, FB), vm(4, 2, 32, FB),
        vm(2, T, FB, t=F32),
        vm(2, T, T, t=F32), vm(16, 8, 2 * T, t=F32), vm(8, 2 * T, t=F32), vm(4, 8, 2 * T, t=F32), vm(8, 8 * CAP, FB),
        vm(4, 8 * CAP, SL, t=F32), vm(2, 8 * CAP, SL), vm(2, 8 * CAP, SL), vm(2, 8 * CAP, SL),
        vm(8, 8 * CAP, FB), vm(2, 4, 4, CAP, FB), vm(2, 4, CAP, FB), vm(3, CAP, FB), vm(8, 3, CAP, FB),
        vm(2, CAP, FB, t=F32), vm(4, T, OUT), vm(4, T, OUT),
        dma(5), dma(4), dma(4), dma(7), dma(7), dma(7), dma(7),
        dma(6), dma(6), dma(2, 8), dma(2, 8), dma(3), dma(3), dma(16), dma(16), dma(3), dma(3),
        dma(2), dma(2), dma(3), dma(3), dma(2, 4, 4), dma(2, 4, 4), dma(2, 4), dma(2, 4), dma(8, 3), dma(8, 3),
        dma(3), dma(3), dma(2, 4, 4), dma(2, 4, 4), dma(2, 4), dma(2, 4), dma(8, 3), dma(8, 3), dma(4), dma(4),
    ]
    return pl.pallas_call(
        kernel,
        out_shape=jax.ShapeDtypeStruct((T, OUT), BF),
        in_specs=[
            outside, inside, inside, inside, inside, inside, inside,
            outside, inside, outside, inside, outside, outside,
        ],
        out_specs=inside,
        scratch_shapes=scratch,
        compiler_params=pltpu.CompilerParams(
            collective_id=0, has_side_effects=True, vmem_limit_bytes=56 * 2**20
        ),
        cost_estimate=pl.CostEstimate(flops=4 * 10**9, bytes_accessed=10**7, transcendentals=10**5),
    )(tok, q, kk, v, ld, inc, ag.reshape(2, HD), wo, fg.reshape(D // 128, 128), ro, ids, wi, wd)


def solution(mesh):
    return jax.shard_map(
        local,
        mesh=mesh,
        in_specs=(
            P("ctx", None),
            P("ctx", "exp"),
            P("ctx", "exp"),
            P("ctx", "exp"),
            P("exp", "ctx"),
            P("exp", None, None),
            P("exp"),
            P("exp", None),
            P(),
            P(),
            P("ctx", None),
            P(None, ("exp", "ctx"), None),
            P(("exp", "ctx"), None),
        ),
        out_specs=P("ctx", "exp"),
        check_vma=False,
    )
```

time: 556 us -> 136 us (0.24)
  the two profiles are of different devices: /device:TPU:1 before, /device:TPU:11 now
where the time goes in v1:
time: 136 us
  Pallas kernels  130 us (96%)
  local copies, waits for them, and re-layouts  5.29 us (4%)
    pallas_call x1, Pallas kernels, local(): pl.pallas_call(kernel, out_shape=jax.ShapeDtypeStruct((T, OUT), BF), in_s...  130 us
    unnamed x2, local copies, waits for them, and re-layouts  3.73 us

profile of v1, /device:TPU:11, one launch (start us, length us, event | category | flops | bytes accessed | tf_op | source)
XLA Modules:
  0.0 135.5 jit_solution(17059689198810220988)
XLA Ops:
  0.0 1.4 %copy.15.ids_ref = s32[128,2]{1,0:T(8,128)} copy(s32[128,2]{0,1:T(2,128)} %param.23) | data formatting | bytes 2048 | tf_op args[10]
  1.4 2.3 %copy.14.ro_ref = bf16[6144,4]{1,0:T(8,128)(2,1)} copy(bf16[6144,4]{0,1:T(4,128)(2,1)} %param.22) | data formatting | bytes 98304 | tf_op args[9]
  3.7 130.2 %shard_map.127 = bf16[128,192]{1,0:T(8,128)(2,1)} custom-call(bf16[128,6144]{1,0:T(8,128)(2,1)} %tok_ref.1, bf16[128,256]{1,0:T(8,128)(2,1)} %q_ref.1, bf16[128,256]{1,0:T(8,128)(2,1)} %k_ref.1, bf16[128,256]{1,0:T(8,128)(2,1)} %v_ref.1, f32[2,128]{1,0:T(2,128)} %ld_ref.1, f32[2,128,128]{2,1,0:T(8,128)} %inc_ref.1, f32[2,128]{1,0:T(2,128)} %bitcast.3, ...), custom_call_target="tpu_custom_call" | custom-call | flops 4000000000 | bytes 10000000 | tf_op jit(solution)/shard_map/pallas_call | solution.py:590
  134.0 1.6 %copy.16 = bf16[128,192]{0,1:T(8,128)(2,1)} copy(bf16[128,192]{1,0:T(8,128)(2,1)} %shard_map.127) | data formatting | bytes 98304 | tf_op jit(solution)/shard_map/pallas_call | solution.py:590

commit v2 on v1

--- a/solution.py
+++ b/solution.py
@@ -21,6 +21,9 @@
 HALF = D // 2
 FB = HALF // 8
 OUT = D // 32
+FZ = 128
+FY = FB - FZ
+DY = 16 * FY
 
 HOPS = ((4, 4, 3, 3), (3, 3, 4, 4))
 HOPB = (4, 3)
@@ -55,13 +58,13 @@
     wi_ref,
     wd_ref,
     out_ref,
-    WO, WI, WD, RO, TK, IDS,
-    LS, TS, LB, TB, ST, WR,
-    AH, PP, A1R, QQ, A2R, A3R, MID,
-    PL, SR, LG, RX, XG, ACC, PS, PR, HID,
+    WO, WI, WD, TK, IDS,
+    LF, LS, TS, LB, TB, ST, SO, LC, TC, IN, QS, WR,
+    AH, PP, PZ, A1R, QQ, A2R, Z1R, ZQ, Z2R, A3R, MID,
+    PL, PT, GC, SR, LG, RX, XG, ACC, PS, PR, HID,
     YY, RBA, RBB, XRA, XRB, YS, FS, FR,
     loc, sib_s, sib_r, st_s, st_r, tt_s, tt_r,
-    a1_s, a1_r, a2_s, a2_r, a3_s, a3_r, sx_s, sx_r, rx_s, rx_r,
+    a1_s, a1_r, z1_s, z1_r, z2_s, z2_r, a2_s, a2_r, a3_s, a3_r, sx_s, sx_r, rx_s, rx_r,
     pr_s, pr_r, ax_s, ax_r, ar_s, ar_r, br_s, br_r, bx_s, bx_r,
     ra_s, ra_r, rr_s, rr_r, rb_s, rb_r, rx2_s, rx2_r, fn_s, fn_r,
 ):
@@ -69,7 +72,11 @@
     e = lax.axis_index("exp")
     x, k = c // 2, lax.rem(c, 2)
     y, z = e // 8, lax.rem(e, 8)
-    b = k * 8 + z
+
+    def pos(zs):
+        return lax.rem(zs, 2) * 4 + zs // 2
+
+    b = k * 8 + pos(z)
     pend = []
 
     def xx(d):
@@ -114,7 +121,8 @@
         hello(c, y * 8 + zz(o))
         hello(sibling, y * 8 + zz(o))
     src_b = e // 2
-    src_k, src_z = src_b // 8, lax.rem(src_b, 8)
+    src_k, src_p = src_b // 8, lax.rem(src_b, 8)
+    src_z = 2 * lax.rem(src_p, 4) + src_p // 4
     src_mine = (src_k == k) & (src_z == z)
     for yy in range(4):
         @pl.when(jnp.logical_not(src_mine & (y == yy)))
@@ -124,10 +132,6 @@
     lc_wo.start()
     lc_tk = pltpu.make_async_copy(tok_ref.at[:, cols(b, FB)], TK.at[k], loc.at[1])
     lc_tk.start()
-    lc_ro = pltpu.make_async_copy(
-        ro_ref.at[pl.ds(pl.multiple_of(b * FB, 16), FB)], RO, loc.at[2]
-    )
-    lc_ro.start()
 
     row_i = iota2((T, T), 0)
     col_i = iota2((T, T), 1)
@@ -141,25 +145,18 @@
         tot = jnp.sum(ld, axis=1, keepdims=True)
         cums.append(cum)
         ks = k_ref[:, hs].astype(F32) * jnp.exp(tot - cum)
-        LS[h] = nn(ks.T, v_ref[:, hs].astype(F32), HI).astype(BF)
+        LF[h] = nn(ks.T, v_ref[:, hs].astype(F32), HI)
+        LS[h] = LF[h].astype(BF)
         TS[h:h + 1, :] = jnp.broadcast_to(tot, (1, T))
     TS[2:, :] = jnp.zeros((6, T), F32)
-    idc = ids_ref[...].astype(F32)
-    ident = row_i == col_i
-    r0 = jnp.sum(jnp.where(ident, idc[:, 0:1], 0.0), axis=0, keepdims=True)
-    r1 = jnp.sum(jnp.where(ident, idc[:, 1:2], 0.0), axis=0, keepdims=True)
-    sub8 = iota2((8, T), 0)
-    IDS[k] = jnp.where(sub8 == 0, r0, jnp.where(sub8 == 1, r1, 0.0))
+    IDS[k, 0:2, :] = ids_ref[...].astype(F32)
+    IDS[k, 2:8, :] = jnp.zeros((6, T), F32)
 
     pl.semaphore_wait(bar, 28 - (src_mine).astype(jnp.int32))
 
-    for d in range(1, 8):
-        @pl.when(c + d < 8)
-        def _(d=d):
-            send(TS, TB.at[d - 1], tt_s.at[d - 1], tt_r.at[d - 1], c + d, e, False)
-            send(LS, LB.at[d - 1], st_s.at[d - 1], st_r.at[d - 1], c + d, e, False)
-
-    ob = (1 - k) * 8 + z
+    send(TS, TB.at[0], tt_s.at[0], tt_r.at[0], sibling, e)
+    send(LS.at[1 - k], LB.at[0], st_s.at[0], st_r.at[0], sibling, e)
+    ob = (1 - k) * 8 + pos(z)
     send(tok_ref.at[:, cols(ob, FB)], TK.at[k], sib_s.at[0], sib_r.at[0], sibling, e)
     send(IDS.at[k], IDS.at[k], sib_s.at[1], sib_r.at[1], sibling, e)
     mine, other = cols(k, HALF), cols(1 - k, HALF)
@@ -170,7 +167,23 @@
     send(wi_ref.at[:, :, other], WI.at[k], sib_s.at[2], sib_r.at[2], sibling, e)
     send(wd_ref.at[:, other], WD.at[k], sib_s.at[3], sib_r.at[3], sibling, e)
 
-    intra, qsc = [], []
+    arrive(TB.at[0], tt_s.at[0], tt_r.at[0])
+    arrive(LB.at[0], st_s.at[0], st_r.at[0])
+    mine_l, other_l = LF[k], LB[0].astype(F32)
+    mine_t, other_t = TS[pl.ds(k, 1), :], TB[0, pl.ds(k, 1), :]
+    core0 = k == 0
+    l0 = jnp.where(core0, mine_l, other_l)
+    l1 = jnp.where(core0, other_l, mine_l)
+    t0 = jnp.where(core0, mine_t, other_t)
+    t1 = jnp.where(core0, other_t, mine_t)
+    LC[...] = (jnp.exp(t1) * l0 + l1).astype(BF)
+    TC[...] = jnp.broadcast_to(t0 + t1, (8, T))
+    for d in range(1, 4):
+        @pl.when(x + d < 4)
+        def _(d=d):
+            send(TC, TB.at[d], tt_s.at[d], tt_r.at[d], c + 2 * d, e, False)
+            send(LC, LB.at[d], st_s.at[d], st_r.at[d], c + 2 * d, e, False)
+
     for h in range(2):
         hs = slice(h * HD, (h + 1) * HD)
         cum = cums[h]
@@ -178,62 +191,88 @@
         gap = jnp.where(lower, cb - cb.T, 0.0)
         weight = jnp.where(lower, jnp.exp(gap), 0.0)
         sc = nt(q_ref[:, hs], k_ref[:, hs]) * scale * weight
-        intra.append(nn(sc, v_ref[:, hs].astype(F32), HI))
-        qsc.append(q_ref[:, hs].astype(F32) * (scale * jnp.exp(cum)))
-
-    ST[...] = jnp.zeros_like(ST)
+        IN[h] = nn(sc, v_ref[:, hs].astype(F32), HI)
+        QS[h] = q_ref[:, hs].astype(F32) * (scale * jnp.exp(cum))
+
+    ST[k] = jnp.zeros((HD, HD), F32)
     WR[...] = jnp.zeros_like(WR)
-    for d in range(1, 8):
-        @pl.when(c >= d)
+    for d in range(1, 4):
+        @pl.when(x >= d)
         def _(d=d):
-            arrive(TB.at[d - 1], tt_s.at[d - 1], tt_r.at[d - 1])
-            arrive(LB.at[d - 1], st_s.at[d - 1], st_r.at[d - 1])
-            for h in range(2):
-                ST[h] = ST[h] + jnp.exp(WR[h:h + 1, :]) * LB[d - 1, h].astype(F32)
-            WR[...] = WR[...] + TB[d - 1]
-    for h in range(2):
-        hs = slice(h * HD, (h + 1) * HD)
-        state = ST[h] + jnp.exp(WR[h:h + 1, :]) * inc_ref[h]
-        att = intra[h] + nn(qsc[h], state, HI)
+            arrive(TB.at[d], tt_s.at[d], tt_r.at[d])
+            arrive(LB.at[d], st_s.at[d], st_r.at[d])
+            ST[k] = ST[k] + jnp.exp(WR[0:1, :]) * LB[d].astype(F32)
+            WR[...] = WR[...] + TB[d]
+    start = ST[k] + jnp.exp(WR[0:1, :]) * inc_ref[k]
+    after = jnp.exp(t0) * start + l0
+    ST[k] = jnp.where(core0, start, after)
+    SO[...] = jnp.where(core0, after, start)
+    send(SO, ST.at[k], tt_s.at[4], tt_r.at[4], sibling, e)
+
+    def finish(h):
+        att = IN[h] + nn(QS[h], ST[h], HI)
         ms = jnp.mean(att * att, axis=1, keepdims=True)
-        AH[:, hs] = (att * lax.rsqrt(ms + EPS) * ag_ref[h:h + 1, :]).astype(BF)
+        AH[:, pl.ds(pl.multiple_of(h * HD, HD), HD)] = (
+            att * lax.rsqrt(ms + EPS) * ag_ref[pl.ds(h, 1), :]
+        ).astype(BF)
+
+    finish(k)
+    arrive(ST.at[1 - k], tt_s.at[4], tt_r.at[4])
+    finish(1 - k)
 
     lc_wo.wait()
     for kc in range(2):
         def project(i, carry, kc=kc):
-            cs = pl.ds(pl.multiple_of(kc * HALF + i * 512, 128), 512)
-            PP[:, cs] = nn(AH[...], WO[:, cs]).astype(BF)
+            bl = kc * 8 + i
+            r = nn(AH[...], WO[:, cols(bl, FB)]).astype(BF)
+            PP[:, cols(bl, FY)] = r[:, :FY]
+            PZ[:, cols(bl, FZ)] = r[:, FY:]
             return carry
-        lax.fori_loop(0, HALF // 512, project, 0)
+        lax.fori_loop(0, 8, project, 0)
+        cs = slice(kc * 8 * FY, (kc + 1) * 8 * FY)
         for d in (2, 1, 3):
             i = kc * 3 + d - 1
-            cs = slice(kc * HALF, (kc + 1) * HALF)
             send(
                 PP.at[pl.ds(pl.multiple_of(yv(d) * 32, 32), 32), cs],
                 A1R.at[d - 1, :, cs],
                 a1_s.at[i], a1_r.at[i], c, yv(d) * 8 + z,
             )
-    for kc in range(2):
-        cs = slice(kc * HALF, (kc + 1) * HALF)
+        dest = 2 * x + kc
+        for o in (4, 3, 5, 2, 6, 1, 7):
+            send(
+                PZ.at[:, cols(kc * 8 + pos(zz(o)), FZ)],
+                Z1R.at[k, o], z1_s.at[kc, o], z1_r.at[k, o], dest, y * 8 + zz(o),
+            )
+        own = cols(kc * 8 + pos(z), FZ)
+
+        @pl.when(k == kc)
+        def _(own=own):
+            Z1R[k, 0] = PZ[:, own]
+
+        @pl.when(k != kc)
+        def _(own=own, kc=kc, dest=dest):
+            send(PZ.at[:, own], Z1R.at[k, 0], z1_s.at[kc, 0], z1_r.at[k, 0], dest, e, False)
+    for kc in range(2):
+        cs = slice(kc * 8 * FY, (kc + 1) * 8 * FY)
         for d in range(1, 4):
             i = kc * 3 + d - 1
             arrive(A1R.at[d - 1, :, cs], a1_s.at[i], a1_r.at[i])
 
         def add_y(i, carry, kc=kc):
-            s = pl.ds(pl.multiple_of(kc * HALF + i * 512, 128), 512)
+            s = pl.ds(pl.multiple_of(kc * 8 * FY + i * 512, 128), 512)
             acc = PP[pl.ds(pl.multiple_of(y * 32, 32), 32), s].astype(F32)
             for d in range(3):
                 acc = acc + A1R[d, :, s].astype(F32)
             QQ[:, s] = acc.astype(BF)
             return carry
-        lax.fori_loop(0, HALF // 512, add_y, 0)
+        lax.fori_loop(0, 8 * FY // 512, add_y, 0)
         dest = 2 * x + kc
         for o in (4, 3, 5, 2, 6, 1, 7):
             send(
-                QQ.at[:, cols(kc * 8 + zz(o), FB)],
+                QQ.at[:, cols(kc * 8 + pos(zz(o)), FY)],
                 A2R.at[k, o], a2_s.at[kc, o], a2_r.at[k, o], dest, y * 8 + zz(o),
             )
-        own = cols(kc * 8 + z, FB)
+        own = cols(kc * 8 + pos(z), FY)
 
         @pl.when(k == kc)
         def _(own=own):
@@ -243,6 +282,20 @@
         def _(own=own, kc=kc, dest=dest):
             send(QQ.at[:, own], A2R.at[k, 0], a2_s.at[kc, 0], a2_r.at[k, 0], dest, e, False)
 
+    for kc in range(2):
+        @pl.when(k != kc)
+        def _(kc=kc):
+            arrive(Z1R.at[kc, 0], z1_s.at[kc, 0], z1_r.at[kc, 0])
+        acc = Z1R[kc, 0].astype(F32)
+        for o in range(1, 8):
+            arrive(Z1R.at[kc, o], z1_s.at[kc, o], z1_r.at[kc, o])
+            acc = acc + Z1R[kc, o].astype(F32)
+        ZQ[kc] = acc.astype(BF)
+    for d in (2, 1, 3):
+        send(
+            ZQ.at[:, pl.ds(pl.multiple_of(yv(d) * 32, 32), 32)], Z2R.at[d - 1],
+            z2_s.at[d - 1], z2_r.at[d - 1], c, yv(d) * 8 + z,
+        )
     for kc in range(2):
         @pl.when(k != kc)
         def _(kc=kc):
@@ -251,7 +304,12 @@
         for o in range(1, 8):
             arrive(A2R.at[kc, o], a2_s.at[kc, o], a2_r.at[kc, o])
             acc = acc + A2R[kc, o].astype(F32)
-        A3R[0, kc] = acc.astype(BF)
+        A3R[0, kc, :, :FY] = acc.astype(BF)
+    acc = ZQ[:, pl.ds(pl.multiple_of(y * 32, 32), 32), :].astype(F32)
+    for d in range(1, 4):
+        arrive(Z2R.at[d - 1], z2_s.at[d - 1], z2_r.at[d - 1])
+        acc = acc + Z2R[d - 1].astype(F32)
+    A3R[0, :, :, FY:] = acc.astype(BF)
     for d in range(1, 4):
         send(A3R.at[0], A3R.at[d], a3_s.at[d - 1], a3_r.at[d - 1], c, yv(d) * 8 + z)
 
@@ -267,7 +325,6 @@
 
     lc_tk.wait()
     arrive(TK.at[1 - k], sib_s.at[0], sib_r.at[0])
-    lc_ro.wait()
     gain = jnp.concatenate([fg_ref[pl.ds(b * 3 + i, 1), :] for i in range(3)], axis=1)
     for d in range(4):
         if d:
@@ -322,14 +379,13 @@
             alpha_ring(0, 0, 1)
             alpha_ring(1, 0, 1)
             beta_x(0)
-    lane = iota2((T, T), 1)
+    router = ro_ref[:, cols(b, FB)]
     for kc in range(2):
         m = MID[kc]
-        lg = nn((m * gain).astype(BF), RO[...])
-        st = jnp.where(lane == 4, jnp.sum(m * m, axis=1, keepdims=True), 0.0)
-        for j in range(4):
-            st = jnp.where(lane == j, lg[:, j:j + 1], st)
-        SR[0, :, kc * T:(kc + 1) * T] = st.T[0:8, :]
+        ts = slice(kc * T, (kc + 1) * T)
+        SR[0, 0:4, ts] = nt(router, (m * gain).astype(BF))
+        square = jnp.sum(m * m, axis=1, keepdims=True)
+        SR[0, 4:8, ts] = jnp.broadcast_to(square, (T, T)).T[0:4, :]
     for o in range(16):
         if o:
             dk = o // 8
@@ -343,7 +399,7 @@
 
     def ffn_in(o, first=False):
         zs = zz(o)
-        ws = cols(zs, FB)
+        ws = cols(pos(zs), FB)
 
         def body(i, carry):
             rows = pl.ds(pl.multiple_of(i * 160, 16), 160)
@@ -381,6 +437,11 @@
         if h == 1:
             beta_x_wait(0)
             ffn_in(0, True)
+        else:
+            for o in (h - 1, 1 - h):
+                beta_x_wait(o)
+                ffn_in(o)
+        if h == 3:
             for o in range(1, 16):
                 arrive(SR.at[o], sx_s.at[o], sx_r.at[o])
             tot = SR[0]
@@ -398,16 +459,37 @@
             RX[0] = rs
             for d in range(1, 4):
                 send(RX.at[0], RX.at[d], rx_s.at[d - 1], rx_r.at[d - 1], 2 * xx(d) + k, e)
-        else:
-            for o in (h - 1, 1 - h):
-                beta_x_wait(o)
-                ffn_in(o)
     beta_x_wait(-4)
-    ffn_in(-4)
-
-    for g in range(2):
-        PS[g] = ACC[2 * (1 - k) + g].astype(BF)
+    ws4 = cols(pos(zz(4)), FB)
+
+    def last(i, carry):
+        rows = pl.ds(pl.multiple_of(i * 160, 16), 160)
+        for g in range(2):
+            r = nt(XG[zz(4), rows, :], WI[1 - k, g, :, ws4])
+            PS[g, rows, :] = (ACC[2 * (1 - k) + g, rows, :] + r).astype(BF)
+        return carry
+    lax.fori_loop(0, 4, last, 0)
+
     send(PS, PR, pr_s.at[0], pr_r.at[0], sibling, e)
+
+    def last_own(i, carry):
+        rows = pl.ds(pl.multiple_of(i * 160, 16), 160)
+        for g in range(2):
+            r = nt(XG[zz(4), rows, :], WI[k, g, :, ws4])
+            ACC[2 * k + g, rows, :] = ACC[2 * k + g, rows, :] + r
+        return carry
+    lax.fori_loop(0, 4, last_own, 0)
+    for kc in range(2):
+        sg = 1.0 / (1.0 + jnp.exp(-LG[:, kc * T:(kc + 1) * T]))
+        i0, i1 = IDS[kc, 0:1, :], IDS[kc, 1:2, :]
+        den = jnp.zeros((1, T), F32)
+        num = jnp.zeros((1, T), F32)
+        for j in range(4):
+            hit = ((i0 == j) | (i1 == j)).astype(F32) * sg[j:j + 1, :]
+            den = den + hit
+            num = num + jnp.where(y == j, hit, 0.0)
+        GC[kc] = jnp.broadcast_to(num / den, (T, T)).T
+        PT[kc] = PL[kc].T[:, :CAP].astype(BF)
     for d in range(1, 4):
         arrive(RX.at[d], rx_s.at[d - 1], rx_r.at[d - 1])
     lc_wd.wait()
@@ -421,12 +503,15 @@
             g = (ACC[2 * k, rows, :] + PR[0, rows, :].astype(F32)) * col
             u = (ACC[2 * k + 1, rows, :] + PR[1, rows, :].astype(F32)) * col
             HID[k, rows, :] = (g / (1.0 + jnp.exp(-g)) * u).astype(BF)
-    send(HID.at[k], HID.at[k], pr_s.at[1], pr_r.at[1], sibling, e)
-    arrive(HID.at[1 - k], pr_s.at[1], pr_r.at[1])
+        part = HID.at[k, pl.ds(pl.multiple_of(xx(-d) * 160, 16), 160)]
+        send(part, part, pr_s.at[1 + d], pr_r.at[1 + d], sibling, e)
+    for d in range(4):
+        part = HID.at[1 - k, pl.ds(pl.multiple_of(xx(-d) * 160, 16), 160)]
+        arrive(part, pr_s.at[1 + d], pr_r.at[1 + d])
 
     def down(o):
         zs = zz(o)
-        ws = cols(zs, FB)
+        ws = cols(pos(zs), FB)
 
         def body(i, carry):
             rows = pl.ds(pl.multiple_of(i * 160, 16), 160)
@@ -475,14 +560,13 @@
                 if (step_dir[r] * HOPS[r][d] - o) % 8 == 0:
                     back_ring(r, d, 0)
         back_x(o)
-    for s in range(1, 5):
-        for d in range(4):
+    for s in range(1, 4):
+        for d in (2, 1, 3, 0):
             for r in range(2):
                 if s < HOPS[r][d]:
                     back_ring(r, d, s)
         for r in range(2):
-            if s - 1 < HOPB[r]:
-                back_ring_b(r, s - 1)
+            back_ring_b(r, s - 1)
     for d in (2, 1, 3, 0):
         acc = YY[z, rows_a(xx(d)), :].astype(F32)
         for r in range(2):
@@ -494,34 +578,25 @@
             p[...] = acc.astype(BF)
             send(p, XRA.at[d - 1], ra_s.at[d - 1], ra_r.at[d - 1], 2 * xx(d) + k, e)
         else:
-            YS[0, :CAP, :] = acc
+            YS[0, :, :] = acc
+    back_ring_b(0, 3)
     acc = back_x_sum(0)
     for r in range(2):
         s = HOPB[r] - 1
         arrive(RBB.at[r, s], rb_s.at[r, s], rb_r.at[r, s])
         acc = acc + RBB[r, s].astype(F32)
-    YS[1, :CAP, :] = acc
-    acc = YS[0, :CAP, :]
+    YS[1, :, :] = acc
+    acc = YS[0, :, :]
     for d in range(1, 4):
         arrive(XRA.at[d - 1], ra_s.at[d - 1], ra_r.at[d - 1])
         acc = acc + XRA[d - 1].astype(F32)
-    YS[0, :CAP, :] = acc
+    YS[0, :, :] = acc
 
     first = (y == 0).astype(F32)
     target = 2 * b
-    to_me = (target == e) | (target + 1 == e)
-    for kc in range(2):
-        sg = 1.0 / (1.0 + jnp.exp(-LG[:, kc * T:(kc + 1) * T]))
-        i0, i1 = IDS[kc, 0:1, :], IDS[kc, 1:2, :]
-        den = jnp.zeros((1, T), F32)
-        num = jnp.zeros((1, T), F32)
-        for j in range(4):
-            hit = ((i0 == j) | (i1 == j)).astype(F32) * sg[j:j + 1, :]
-            den = den + hit
-            num = num + jnp.where(y == j, hit, 0.0)
-        gate = num / den
-        got = nn((PL[kc] * gate).T[:, :CAP], YS[kc, :CAP, :], HI)
-        got = got + first * MID[kc]
+    for kc in range(2):
+        got = nn(PT[kc], YS[kc].astype(BF))
+        got = got * GC[kc, :, 0:1] + first * MID[kc]
         for j in range(2):
             FS[kc * 2 + j] = got[:, j * OUT:(j + 1) * OUT].astype(BF)
             dc, de = 2 * x + kc, target + j
@@ -552,15 +627,16 @@
 
     for cp in pend:
         cp.wait_send()
-    for d in range(1, 8):
-        @pl.when(c + d < 8)
+    for d in range(1, 4):
+        @pl.when(x + d < 4)
         def _(d=d):
-            left(TS, tt_s.at[d - 1])
-            left(LS, st_s.at[d - 1])
+            left(TC, tt_s.at[d])
+            left(LC, st_s.at[d])
     for kc in range(2):
         @pl.when(k != kc)
         def _(kc=kc):
-            left(QQ.at[:, cols(kc * 8 + z, FB)], a2_s.at[kc, 0])
+            left(QQ.at[:, cols(kc * 8 + pos(z), FY)], a2_s.at[kc, 0])
+            left(PZ.at[:, cols(kc * 8 + pos(z), FZ)], z1_s.at[kc, 0])
         for j in range(2):
             @pl.when(jnp.logical_not((k == kc) & (target + j == e)))
             def _(i=kc * 2 + j):
@@ -573,18 +649,20 @@
     inside = pl.BlockSpec(memory_space=pltpu.VMEM)
     outside = pl.BlockSpec(memory_space=pl.ANY)
     scratch = [
-        vm(256, D), vm(2, 2, SL, HALF), vm(2, SL, HALF), vm(FB, 4), vm(2, T, FB), vm(2, 8, T, t=F32),
-        vm(2, HD, HD), vm(8, T, t=F32), vm(7, 2, HD, HD), vm(7, 8, T, t=F32),
-        vm(2, HD, HD, t=F32), vm(8, T, t=F32),
-        vm(T, 2 * HD), vm(T, D), vm(3, 32, D), vm(32, D), vm(2, 8, 32, FB), vm(4, 2, 32, FB),
+        vm(256, D), vm(2, 2, SL, HALF), vm(2, SL, HALF), vm(2, T, FB), vm(2, 8, T, t=F32),
+        vm(2, HD, HD, t=F32), vm(2, HD, HD), vm(8, T, t=F32), vm(4, HD, HD), vm(4, 8, T, t=F32),
+        vm(2, HD, HD, t=F32), vm(HD, HD, t=F32), vm(HD, HD), vm(8, T, t=F32),
+        vm(2, T, HD, t=F32), vm(2, T, HD, t=F32), vm(8, T, t=F32),
+        vm(T, 2 * HD), vm(T, DY), vm(T, D - DY), vm(3, 32, DY), vm(32, DY), vm(2, 8, 32, FY),
+        vm(2, 8, T, FZ), vm(2, T, FZ), vm(3, 2, 32, FZ), vm(4, 2, 32, FB),
         vm(2, T, FB, t=F32),
-        vm(2, T, T, t=F32), vm(16, 8, 2 * T, t=F32), vm(8, 2 * T, t=F32), vm(4, 8, 2 * T, t=F32), vm(8, 8 * CAP, FB),
+        vm(2, T, T, t=F32), vm(2, T, CAP), vm(2, T, T, t=F32), vm(16, 8, 2 * T, t=F32), vm(8, 2 * T, t=F32), vm(4, 8, 2 * T, t=F32), vm(8, 8 * CAP, FB),
         vm(4, 8 * CAP, SL, t=F32), vm(2, 8 * CAP, SL), vm(2, 8 * CAP, SL), vm(2, 8 * CAP, SL),
         vm(8, 8 * CAP, FB), vm(2, 4, 4, CAP, FB), vm(2, 4, CAP, FB), vm(3, CAP, FB), vm(8, 3, CAP, FB),
         vm(2, CAP, FB, t=F32), vm(4, T, OUT), vm(4, T, OUT),
-        dma(5), dma(4), dma(4), dma(7), dma(7), dma(7), dma(7),
-        dma(6), dma(6), dma(2, 8), dma(2, 8), dma(3), dma(3), dma(16), dma(16), dma(3), dma(3),
-        dma(2), dma(2), dma(3), dma(3), dma(2, 4, 4), dma(2, 4, 4), dma(2, 4), dma(2, 4), dma(8, 3), dma(8, 3),
+        dma(5), dma(4), dma(4), dma(4), dma(4), dma(5), dma(5),
+        dma(6), dma(6), dma(2, 8), dma(2, 8), dma(3), dma(3), dma(2, 8), dma(2, 8), dma(3), dma(3), dma(16), dma(16), dma(3), dma(3),
+        dma(5), dma(5), dma(3), dma(3), dma(2, 4, 4), dma(2, 4, 4), dma(2, 4), dma(2, 4), dma(8, 3), dma(8, 3),
         dma(3), dma(3), dma(2, 4, 4), dma(2, 4, 4), dma(2, 4), dma(2, 4), dma(8, 3), dma(8, 3), dma(4), dma(4),
     ]
     return pl.pallas_call(
@@ -592,7 +670,7 @@
         out_shape=jax.ShapeDtypeStruct((T, OUT), BF),
         in_specs=[
             outside, inside, inside, inside, inside, inside, inside,
-            outside, inside, outside, inside, outside, outside,
+            outside, inside, inside, inside, outside, outside,
         ],
         out_specs=inside,
         scratch_shapes=scratch,
@@ -600,7 +678,7 @@
             collective_id=0, has_side_effects=True, vmem_limit_bytes=56 * 2**20
         ),
         cost_estimate=pl.CostEstimate(flops=4 * 10**9, bytes_accessed=10**7, transcendentals=10**5),
-    )(tok, q, kk, v, ld, inc, ag.reshape(2, HD), wo, fg.reshape(D // 128, 128), ro, ids, wi, wd)
+    )(tok, q, kk, v, ld, inc, ag.reshape(2, HD), wo, fg.reshape(D // 128, 128), ro.T, ids.T, wi, wd)
 
 
 def solution(mesh):

time: 136 us -> 124 us (0.912)
  the two profiles are of different devices: /device:TPU:11 before, /device:TPU:1 now
where the time goes in v2:
time: 124 us
  Pallas kernels  122 us (98%)
  local copies, waits for them, and re-layouts  1.56 us (1%)
    pallas_call x1, Pallas kernels, local(): pl.pallas_call(kernel, out_shape=jax.ShapeDtypeStruct((T, OUT), BF), in_s...  122 us

profile of v2, /device:TPU:1, one launch (start us, length us, event | category | flops | bytes accessed | tf_op | source)
XLA Modules:
  0.0 123.6 jit_solution(16846368620759829236)
XLA Ops:
  0.0 122.1 %shard_map.127 = bf16[128,192]{1,0:T(8,128)(2,1)} custom-call(bf16[128,6144]{1,0:T(8,128)(2,1)} %tok_ref.1, bf16[128,256]{1,0:T(8,128)(2,1)} %q_ref.1, bf16[128,256]{1,0:T(8,128)(2,1)} %k_ref.1, bf16[128,256]{1,0:T(8,128)(2,1)} %v_ref.1, f32[2,128]{1,0:T(2,128)} %ld_ref.1, f32[2,128,128]{2,1,0:T(8,128)} %inc_ref.1, f32[2,128]{1,0:T(2,128)} %bitcast.6, ...), custom_call_target="tpu_custom_call" | custom-call | flops 4000000000 | bytes 10000000 | tf_op jit(solution)/shard_map/pallas_call | solution.py:668
  122.1 1.6 %copy.14 = bf16[128,192]{0,1:T(8,128)(2,1)} copy(bf16[128,192]{1,0:T(8,128)(2,1)} %shard_map.127) | data formatting | bytes 98304 | tf_op jit(solution)/shard_map/pallas_call | solution.py:668

commit v3 on v2

--- a/solution.py
+++ b/solution.py
@@ -27,6 +27,8 @@
 
 HOPS = ((4, 4, 3, 3), (3, 3, 4, 4))
 HOPB = (4, 3)
+NG = 64
+NR = 64
 
 
 def nt(a, b, precision=None):
@@ -113,11 +115,12 @@
         pl.semaphore_signal(bar, inc=1, device_id=(dc, de), device_id_type=MESH)
 
     sibling = 2 * x + (1 - k)
-    for d in range(1, 8):
-        hello(lax.rem(c + d, 8), e)
+    hello(sibling, e)
+    for d in range(1, 4):
+        hello(2 * xx(d) + k, e)
     for d in range(1, 4):
         hello(c, yv(d) * 8 + z)
-    for o in range(1, 8):
+    for o in (4, 3, 5, 2, 6, 1, 7):
         hello(c, y * 8 + zz(o))
         hello(sibling, y * 8 + zz(o))
     src_b = e // 2
@@ -152,7 +155,7 @@
     IDS[k, 0:2, :] = ids_ref[...].astype(F32)
     IDS[k, 2:8, :] = jnp.zeros((6, T), F32)
 
-    pl.semaphore_wait(bar, 28 - (src_mine).astype(jnp.int32))
+    pl.semaphore_wait(bar, 25 - (src_mine).astype(jnp.int32))
 
     send(TS, TB.at[0], tt_s.at[0], tt_r.at[0], sibling, e)
     send(LS.at[1 - k], LB.at[0], st_s.at[0], st_r.at[0], sibling, e)
@@ -333,11 +336,14 @@
         for kc in range(2):
             MID[kc, rows, :] = TK[kc, rows, :].astype(F32) + A3R[d, kc].astype(F32)
 
-    def rows_a(i):
-        return pl.ds(pl.multiple_of(i * 160, 16), 80)
-
-    def rows_b(i):
-        return pl.ds(pl.multiple_of(i * 160 + 80, 16), 80)
+    def rows_a(i, n=NG):
+        return pl.ds(pl.multiple_of(i * 160, 16), n)
+
+    def rows_b(i, n=NG):
+        return pl.ds(pl.multiple_of(i * 160 + n, 16), 160 - n)
+
+    def slot_rows(i, kc):
+        return pl.ds(pl.multiple_of(i * 160 + 80 * kc, 16), 80)
 
     def piece_a(zs, d):
         return XG.at[zs, rows_a(xx(-d))]
@@ -367,33 +373,19 @@
     for kc in (1, 0):
         xg = (MID[kc] * gain).astype(BF)
         slots = nn(PL[kc, :CAP, :].astype(BF), xg).astype(BF)
-        if kc:
-            XG[z, rows_b(x), :] = slots
+        XG[z, slot_rows(x, kc), :] = slots
+        if kc and NG >= 80:
             beta_ring(0, 1)
             beta_ring(1, 1)
-        else:
-            XG[z, rows_a(x), :] = slots
-            pa = piece_a(z, 0)
-            for d in range(1, 4):
-                send(pa, pa, ax_s.at[d - 1], ax_r.at[d - 1], 2 * xx(d) + k, e)
-            alpha_ring(0, 0, 1)
-            alpha_ring(1, 0, 1)
-            beta_x(0)
-    router = ro_ref[:, cols(b, FB)]
-    for kc in range(2):
-        m = MID[kc]
-        ts = slice(kc * T, (kc + 1) * T)
-        SR[0, 0:4, ts] = nt(router, (m * gain).astype(BF))
-        square = jnp.sum(m * m, axis=1, keepdims=True)
-        SR[0, 4:8, ts] = jnp.broadcast_to(square, (T, T)).T[0:4, :]
-    for o in range(16):
-        if o:
-            dk = o // 8
-            send(
-                SR.at[0], SR.at[o], sx_s.at[o], sx_r.at[o],
-                sibling if dk else c, y * 8 + zz(o % 8),
-            )
-
+    if NG < 80:
+        beta_ring(0, 1)
+        beta_ring(1, 1)
+    pa = piece_a(z, 0)
+    for d in range(1, 4):
+        send(pa, pa, ax_s.at[d - 1], ax_r.at[d - 1], 2 * xx(d) + k, e)
+    alpha_ring(0, 0, 1)
+    alpha_ring(1, 0, 1)
+    beta_x(0)
     lc_wi.wait()
     arrive(WI.at[1 - k], sib_s.at[2], sib_r.at[2])
 
@@ -441,7 +433,23 @@
             for o in (h - 1, 1 - h):
                 beta_x_wait(o)
                 ffn_in(o)
-        if h == 3:
+        if h == 2:
+            router = ro_ref[:, cols(b, FB)]
+            for kc in range(2):
+                m = MID[kc]
+                ts = slice(kc * T, (kc + 1) * T)
+                SR[0, 0:4, ts] = nt(router, (m * gain).astype(BF))
+                square = jnp.sum(m * m, axis=1, keepdims=True)
+                SR[0, 4:8, ts] = jnp.broadcast_to(square, (T, T)).T[0:4, :]
+            for o in range(16):
+                if o:
+                    dk = o // 8
+                    send(
+                        SR.at[0], SR.at[o], sx_s.at[o], sx_r.at[o],
+                        sibling if dk else c, y * 8 + zz(o % 8),
+                    )
+
+        if h == 4:
             for o in range(1, 16):
                 arrive(SR.at[o], sx_s.at[o], sx_r.at[o])
             tot = SR[0]
@@ -499,7 +507,7 @@
         for kc in range(2):
             rs = RX[d, 0:1, kc * T:(kc + 1) * T]
             col = jnp.broadcast_to(rs, (T, T)).T[:CAP, 0:1]
-            rows = (rows_b if kc else rows_a)(xx(-d))
+            rows = slot_rows(xx(-d), kc)
             g = (ACC[2 * k, rows, :] + PR[0, rows, :].astype(F32)) * col
             u = (ACC[2 * k + 1, rows, :] + PR[1, rows, :].astype(F32)) * col
             HID[k, rows, :] = (g / (1.0 + jnp.exp(-g)) * u).astype(BF)
@@ -523,7 +531,7 @@
     def back_ring(r, d, s):
         hops = HOPS[r][d]
         zs = zz(step_dir[r] * (hops - s))
-        p = YY.at[zs, rows_a(xx(d))]
+        p = YY.at[zs, rows_a(xx(d), NR)]
         if s:
             arrive(RBA.at[r, d, s - 1], rr_s.at[r, d, s - 1], rr_r.at[r, d, s - 1])
             p[...] = (p[...].astype(F32) + RBA[r, d, s - 1].astype(F32)).astype(BF)
@@ -532,12 +540,12 @@
     def back_x(o):
         for d in range(1, 4):
             send(
-                YY.at[zz(o), rows_b(xx(d))], XRB.at[o % 8, d - 1],
+                YY.at[zz(o), rows_b(xx(d), NR)], XRB.at[o % 8, d - 1],
                 rx2_s.at[o % 8, d - 1], rx2_r.at[o % 8, d - 1], 2 * xx(d) + k, e,
             )
 
     def back_x_sum(o):
-        acc = YY[zz(o), rows_b(x), :].astype(F32)
+        acc = YY[zz(o), rows_b(x, NR), :].astype(F32)
         for d in range(1, 4):
             arrive(XRB.at[o % 8, d - 1], rx2_s.at[o % 8, d - 1], rx2_r.at[o % 8, d - 1])
             acc = acc + XRB[o % 8, d - 1].astype(F32)
@@ -549,7 +557,7 @@
         if s:
             arrive(RBB.at[r, s - 1], rb_s.at[r, s - 1], rb_r.at[r, s - 1])
             acc = acc + RBB[r, s - 1].astype(F32)
-        p = YY.at[zz(o), rows_b(x)]
+        p = YY.at[zz(o), rows_b(x, NR)]
         p[...] = acc.astype(BF)
         send(p, RBB.at[r, s], rb_s.at[r, s], rb_r.at[r, s], c, y * 8 + zz(step_dir[r]))
 
@@ -568,34 +576,34 @@
         for r in range(2):
             back_ring_b(r, s - 1)
     for d in (2, 1, 3, 0):
-        acc = YY[z, rows_a(xx(d)), :].astype(F32)
+        acc = YY[z, rows_a(xx(d), NR), :].astype(F32)
         for r in range(2):
             s = HOPS[r][d] - 1
             arrive(RBA.at[r, d, s], rr_s.at[r, d, s], rr_r.at[r, d, s])
             acc = acc + RBA[r, d, s].astype(F32)
         if d:
-            p = YY.at[z, rows_a(xx(d))]
+            p = YY.at[z, rows_a(xx(d), NR)]
             p[...] = acc.astype(BF)
             send(p, XRA.at[d - 1], ra_s.at[d - 1], ra_r.at[d - 1], 2 * xx(d) + k, e)
         else:
-            YS[0, :, :] = acc
+            YS[:NR, :] = acc
     back_ring_b(0, 3)
     acc = back_x_sum(0)
     for r in range(2):
         s = HOPB[r] - 1
         arrive(RBB.at[r, s], rb_s.at[r, s], rb_r.at[r, s])
         acc = acc + RBB[r, s].astype(F32)
-    YS[1, :, :] = acc
-    acc = YS[0, :, :]
+    YS[NR:, :] = acc
+    acc = YS[:NR, :]
     for d in range(1, 4):
         arrive(XRA.at[d - 1], ra_s.at[d - 1], ra_r.at[d - 1])
         acc = acc + XRA[d - 1].astype(F32)
-    YS[0, :, :] = acc
+    YS[:NR, :] = acc
 
     first = (y == 0).astype(F32)
     target = 2 * b
     for kc in range(2):
-        got = nn(PT[kc], YS[kc].astype(BF))
+        got = nn(PT[kc], YS[kc * CAP:(kc + 1) * CAP, :].astype(BF))
         got = got * GC[kc, :, 0:1] + first * MID[kc]
         for j in range(2):
             FS[kc * 2 + j] = got[:, j * OUT:(j + 1) * OUT].astype(BF)
@@ -658,8 +666,8 @@
         vm(2, T, FB, t=F32),
         vm(2, T, T, t=F32), vm(2, T, CAP), vm(2, T, T, t=F32), vm(16, 8, 2 * T, t=F32), vm(8, 2 * T, t=F32), vm(4, 8, 2 * T, t=F32), vm(8, 8 * CAP, FB),
         vm(4, 8 * CAP, SL, t=F32), vm(2, 8 * CAP, SL), vm(2, 8 * CAP, SL), vm(2, 8 * CAP, SL),
-        vm(8, 8 * CAP, FB), vm(2, 4, 4, CAP, FB), vm(2, 4, CAP, FB), vm(3, CAP, FB), vm(8, 3, CAP, FB),
-        vm(2, CAP, FB, t=F32), vm(4, T, OUT), vm(4, T, OUT),
+        vm(8, 8 * CAP, FB), vm(2, 4, 4, NR, FB), vm(2, 4, 160 - NR, FB), vm(3, NR, FB), vm(8, 3, 160 - NR, FB),
+        vm(160, FB, t=F32), vm(4, T, OUT), vm(4, T, OUT),
         dma(5), dma(4), dma(4), dma(4), dma(4), dma(5), dma(5),
         dma(6), dma(6), dma(2, 8), dma(2, 8), dma(3), dma(3), dma(2, 8), dma(2, 8), dma(3), dma(3), dma(16), dma(16), dma(3), dma(3),
         dma(5), dma(5), dma(3), dma(3), dma(2, 4, 4), dma(2, 4, 4), dma(2, 4), dma(2, 4), dma(8, 3), dma(8, 3),

time: 124 us -> 121 us (0.976)
  Pallas kernels: 122 us -> 119 us
    pallas_call x1, Pallas kernels: 122 us -> 119 us  [local(): pl.pallas_call(kernel, out_shape=jax.ShapeDtypeStruct((T, OUT), BF), in_s...]
where the time goes in v3:
time: 121 us
  Pallas kernels  119 us (98%)
  local copies, waits for them, and re-layouts  1.56 us (1%)
    pallas_call x1, Pallas kernels, local(): pl.pallas_call(kernel, out_shape=jax.ShapeDtypeStruct((T, OUT), BF), in_s...  119 us

profile of v3, /device:TPU:1, one launch (start us, length us, event | category | flops | bytes accessed | tf_op | source)
XLA Modules:
  0.0 121.1 jit_solution(7682663861348970232)
XLA Ops:
  0.0 119.5 %shard_map.127 = bf16[128,192]{1,0:T(8,128)(2,1)} custom-call(bf16[128,6144]{1,0:T(8,128)(2,1)} %tok_ref.1, bf16[128,256]{1,0:T(8,128)(2,1)} %q_ref.1, bf16[128,256]{1,0:T(8,128)(2,1)} %k_ref.1, bf16[128,256]{1,0:T(8,128)(2,1)} %v_ref.1, f32[2,128]{1,0:T(2,128)} %ld_ref.1, f32[2,128,128]{2,1,0:T(8,128)} %inc_ref.1, f32[2,128]{1,0:T(2,128)} %bitcast.6, ...), custom_call_target="tpu_custom_call" | custom-call | flops 4000000000 | bytes 10000000 | tf_op jit(solution)/shard_map/pallas_call | solution.py:676
  119.5 1.6 %copy.14 = bf16[128,192]{0,1:T(8,128)(2,1)} copy(bf16[128,192]{1,0:T(8,128)(2,1)} %shard_map.127) | data formatting | bytes 98304 | tf_op jit(solution)/shard_map/pallas_call | solution.py:676

commit v4 on v3

--- a/solution.py
+++ b/solution.py
@@ -363,7 +363,7 @@
 
     def beta_x(o):
         p = piece_b(zz(o), 0)
-        for d in range(1, 4):
+        for d in (2, 1, 3):
             send(p, p, bx_s.at[o % 8, d - 1], bx_r.at[o % 8, d - 1], 2 * xx(d) + k, e)
 
     def beta_x_wait(o):
@@ -470,15 +470,14 @@
     beta_x_wait(-4)
     ws4 = cols(pos(zz(4)), FB)
 
-    def last(i, carry):
-        rows = pl.ds(pl.multiple_of(i * 160, 16), 160)
-        for g in range(2):
+    for g in range(2):
+        def last(i, carry, g=g):
+            rows = pl.ds(pl.multiple_of(i * 160, 16), 160)
             r = nt(XG[zz(4), rows, :], WI[1 - k, g, :, ws4])
             PS[g, rows, :] = (ACC[2 * (1 - k) + g, rows, :] + r).astype(BF)
-        return carry
-    lax.fori_loop(0, 4, last, 0)
-
-    send(PS, PR, pr_s.at[0], pr_r.at[0], sibling, e)
+            return carry
+        lax.fori_loop(0, 4, last, 0)
+        send(PS.at[g], PR.at[g], pr_s.at[5 * g], pr_r.at[5 * g], sibling, e)
 
     def last_own(i, carry):
         rows = pl.ds(pl.multiple_of(i * 160, 16), 160)
@@ -502,7 +501,8 @@
         arrive(RX.at[d], rx_s.at[d - 1], rx_r.at[d - 1])
     lc_wd.wait()
     arrive(WD.at[1 - k], sib_s.at[3], sib_r.at[3])
-    arrive(PR, pr_s.at[0], pr_r.at[0])
+    for g in range(2):
+        arrive(PR.at[g], pr_s.at[5 * g], pr_r.at[5 * g])
     for d in range(4):
         for kc in range(2):
             rs = RX[d, 0:1, kc * T:(kc + 1) * T]
@@ -670,7 +670,7 @@
         vm(160, FB, t=F32), vm(4, T, OUT), vm(4, T, OUT),
         dma(5), dma(4), dma(4), dma(4), dma(4), dma(5), dma(5),
         dma(6), dma(6), dma(2, 8), dma(2, 8), dma(3), dma(3), dma(2, 8), dma(2, 8), dma(3), dma(3), dma(16), dma(16), dma(3), dma(3),
-        dma(5), dma(5), dma(3), dma(3), dma(2, 4, 4), dma(2, 4, 4), dma(2, 4), dma(2, 4), dma(8, 3), dma(8, 3),
+        dma(6), dma(6), dma(3), dma(3), dma(2, 4, 4), dma(2, 4, 4), dma(2, 4), dma(2, 4), dma(8, 3), dma(8, 3),
         dma(3), dma(3), dma(2, 4, 4), dma(2, 4, 4), dma(2, 4), dma(2, 4), dma(8, 3), dma(8, 3), dma(4), dma(4),
     ]
     return pl.pallas_call(

time: 121 us -> 121 us (level)
  no operation moved by 1% of the time
where the time goes in v4:
time: 121 us
  Pallas kernels  119 us (98%)
  local copies, waits for them, and re-layouts  1.56 us (1%)
    pallas_call x1, Pallas kernels, local(): pl.pallas_call(kernel, out_shape=jax.ShapeDtypeStruct((T, OUT), BF), in_s...  119 us

profile of v4, /device:TPU:1, one launch (start us, length us, event | category | flops | bytes accessed | tf_op | source)
XLA Modules:
  0.0 120.9 jit_solution(3689843134013616743)
XLA Ops:
  0.0 119.4 %shard_map.127 = bf16[128,192]{1,0:T(8,128)(2,1)} custom-call(bf16[128,6144]{1,0:T(8,128)(2,1)} %tok_ref.1, bf16[128,256]{1,0:T(8,128)(2,1)} %q_ref.1, bf16[128,256]{1,0:T(8,128)(2,1)} %k_ref.1, bf16[128,256]{1,0:T(8,128)(2,1)} %v_ref.1, f32[2,128]{1,0:T(2,128)} %ld_ref.1, f32[2,128,128]{2,1,0:T(8,128)} %inc_ref.1, f32[2,128]{1,0:T(2,128)} %bitcast.6, ...), custom_call_target="tpu_custom_call" | custom-call | flops 4000000000 | bytes 10000000 | tf_op jit(solution)/shard_map/pallas_call | solution.py:676
  119.4 1.6 %copy.14 = bf16[128,192]{0,1:T(8,128)(2,1)} copy(bf16[128,192]{1,0:T(8,128)(2,1)} %shard_map.127) | data formatting | bytes 98304 | tf_op jit(solution)/shard_map/pallas_call | solution.py:676
